TPU v7x, 768 devices: a whole 4x8x12 slice. The times are simulated.
768 devices in a mesh: blk: 24 (over z_hi, x, core), grp: 32 (over y, z_lo).
Axes of the slice: x: 4, y: 8, z: 12 (z_hi: 3, z_lo: 4; z = z_hi * 4 + z_lo), core: 2. Of those that a mesh axis runs over, the one named last changes fastest.
Arguments:
- picture_vectors: bfloat16 [196608, 1152], P(('blk', 'grp')), may hold values from -0.1875 to 0.1875
- sentence_vectors: bfloat16 [196608, 1152], P(('blk', 'grp')), may hold values from -0.1875 to 0.1875
- sharpness_factor: float32 [1], replicated, may hold values from 20 to 60
- additive_shift_term: float32 [1], replicated, may hold values from -3 to 0
- upstream_adjoint: float32 [1], replicated, may hold values from 256 to 1024
Outputs:
- grad_images: bfloat16 [196608, 1152], P(('blk', 'grp'))
- grad_texts: bfloat16 [196608, 1152], P(('blk', 'grp'))
All inputs are finite; a program needn't handle non-finite values.
Results may differ from a plain program's by a relative error of at most 0.0056.
Values may be sent and summed in bfloat16 or wider, within the bound.
A program may use at most 32 MiB of HBM per device.

v0:
```python
import jax
import jax.numpy as jnp
from jax import lax
from jax.sharding import PartitionSpec as P

STEPS = 3


def from_behind(value, axis, steps):
    count = lax.axis_size(axis)
    pairs = [(source, (source + steps) % count) for source in range(count)]
    return lax.ppermute(value, axis, pairs)


def pair_weights(
    local_record_count,
    pending_pieces,
    multiplier_matrix,
    exp_sharpness,
    shifted_affinity,
    identity_selector,
):
    similarity_matrix = lax.dot_general(
        local_record_count,
        pending_pieces,
        (((1,), (1,)), ((), ())),
        preferred_element_type=jnp.float32,
    )
    likelihood_matrix = jax.nn.sigmoid(exp_sharpness * similarity_matrix + shifted_affinity)
    if identity_selector:
        column_entries = lax.broadcasted_iota(jnp.int32, likelihood_matrix.shape, 1)
        row_ids = lax.broadcasted_iota(jnp.int32, likelihood_matrix.shape, 0)
        likelihood_matrix = likelihood_matrix - (column_entries == row_ids).astype(jnp.float32)
    return (multiplier_matrix * likelihood_matrix).astype(jnp.bfloat16)


def on_device(
    picture_vectors, sentence_vectors, sharpness_factor, additive_shift_term, upstream_adjoint
):
    rows = picture_vectors.shape[0]
    minibatch_size = rows * lax.axis_size("blk") * lax.axis_size("grp")
    exp_sharpness = sharpness_factor[0]
    shifted_affinity = additive_shift_term[0]
    multiplier_matrix = upstream_adjoint[0] * exp_sharpness / minibatch_size
    grad_img = jnp.zeros(picture_vectors.shape, jnp.float32)
    grad_own = jnp.zeros(sentence_vectors.shape, jnp.float32)
    for reach in range(2):
        if reach == 0:
            tile_index = sentence_vectors
        else:
            tile_index = from_behind(sentence_vectors, "grp", 1)
        partials = []
        for step in range(STEPS):
            if step > 0:
                tile_index = from_behind(tile_index, "blk", 1)
            initial_flag = step == 0 and reach == 0
            weight_factors = pair_weights(
                picture_vectors,
                tile_index,
                multiplier_matrix,
                exp_sharpness,
                shifted_affinity,
                initial_flag,
            )
            grad_img = grad_img + jnp.dot(
                weight_factors, tile_index, preferred_element_type=jnp.float32
            )
            partials.append(
                lax.dot_general(
                    weight_factors,
                    picture_vectors,
                    (((0,), (0,)), ((), ())),
                    preferred_element_type=jnp.float32,
                )
            )
        carried = partials[STEPS - 1]
        for step in range(STEPS - 2, -1, -1):
            carried = (
                from_behind(carried.astype(jnp.bfloat16), "blk", -1).astype(jnp.float32)
                + partials[step]
            )
        if reach == 1:
            carried = from_behind(carried.astype(jnp.bfloat16), "grp", -1).astype(jnp.float32)
        grad_own = grad_own + carried
    return (grad_img.astype(jnp.bfloat16), grad_own.astype(jnp.bfloat16))


def solution(mesh):
    return jax.shard_map(
        on_device,
        mesh=mesh,
        in_specs=(P(("blk", "grp"), None), P(("blk", "grp"), None), P(), P(), P()),
        out_specs=(P(("blk", "grp"), None), P(("blk", "grp"), None)),
        check_vma=False,
    )
```

profile of v0, /device:TPU:577, one launch (start us, length us, event | category | flops | bytes accessed | tf_op | source)
XLA Modules:
  0.0 240.6 jit_solution(8392572498622733897)
XLA Ops:
  0.6 3.2 %collective-permute-start.2 = (bf16[256,1152]{1,0:T(8,128)(2,1)}, bf16[256,1152]{1,0:T(8,128)(2,1)S(1)}, u32[]{:S(2)}, u32[]{:S(2)}) collective-permute-start(bf16[256,1152]{1,0:T(8,128)(2,1)} %param.6), channel_id=1, source_target_pairs={{0,1},{1,2},{2,3},{3,4},{4,5},{5,6},{6,7},{7,8},{8,9},{9,10},{10,1... | collective-permute-start | bytes 1769480 | tf_op jit(solution)/shard_map/ppermute | solution.py:12
  3.9 4.0 %collective-permute-start = (bf16[256,1152]{1,0:T(8,128)(2,1)}, bf16[256,1152]{1,0:T(8,128)(2,1)S(1)}, u32[]{:S(2)}, u32[]{:S(2)}) collective-permute-start(bf16[256,1152]{1,0:T(8,128)(2,1)} %param.6), channel_id=1, source_target_pairs={{0,32},{32,64},{64,96},{96,128},{128,160},{160,192},{192,224},{224... | collective-permute-start | bytes 1769480 | tf_op jit(solution)/shard_map/ppermute | solution.py:12
  9.8 7.3 %collective-permute-done.2 = bf16[256,1152]{1,0:T(8,128)(2,1)S(1)} collective-permute-done((bf16[256,1152]{1,0:T(8,128)(2,1)}, bf16[256,1152]{1,0:T(8,128)(2,1)S(1)}, u32[]{:S(2)}, u32[]{:S(2)}) %collective-permute-start.2) | collective-permute-done | bytes 589856 | tf_op jit(solution)/shard_map/ppermute | solution.py:12
  17.1 4.5 %collective-permute-start.3 = (bf16[256,1152]{1,0:T(8,128)(2,1)S(1)}, bf16[256,1152]{1,0:T(8,128)(2,1)S(1)}, u32[]{:S(2)}, u32[]{:S(2)}) collective-permute-start(bf16[256,1152]{1,0:T(8,128)(2,1)S(1)} %collective-permute-done.2), channel_id=1, source_target_pairs={{0,32},{32,64},{64,96},{96,128},{128,160},{160,192},{192,224},{224... | collective-permute-start | bytes 1769480 | tf_op jit(solution)/shard_map/ppermute | solution.py:12
  21.6 1.5 fusion.39
  23.5 0.4 fusion.47
  23.9 1.9 collective-permute-start.1
  25.9 2.6 %collective-permute-done.3 = bf16[256,1152]{1,0:T(8,128)(2,1)S(1)} collective-permute-done((bf16[256,1152]{1,0:T(8,128)(2,1)S(1)}, bf16[256,1152]{1,0:T(8,128)(2,1)S(1)}, u32[]{:S(2)}, u32[]{:S(2)}) %collective-permute-start.3) | collective-permute-done | bytes 589856 | tf_op jit(solution)/shard_map/ppermute | solution.py:12
  28.4 4.4 %collective-permute-start.4 = (bf16[256,1152]{1,0:T(8,128)(2,1)S(1)}, bf16[256,1152]{1,0:T(8,128)(2,1)S(1)}, u32[]{:S(2)}, u32[]{:S(2)}) collective-permute-start(bf16[256,1152]{1,0:T(8,128)(2,1)S(1)} %collective-permute-done.3), channel_id=1, source_target_pairs={{0,32},{32,64},{64,96},{96,128},{128,160},{160,192},{192,224},{224... | collective-permute-start | bytes 1769480 | tf_op jit(solution)/shard_map/ppermute | solution.py:12
  32.8 0.4 fusion.42
  33.9 25.8 %collective-permute-done.4 = bf16[256,1152]{1,0:T(8,128)(2,1)S(1)} collective-permute-done((bf16[256,1152]{1,0:T(8,128)(2,1)S(1)}, bf16[256,1152]{1,0:T(8,128)(2,1)S(1)}, u32[]{:S(2)}, u32[]{:S(2)}) %collective-permute-start.4) | collective-permute-done | bytes 589856 | tf_op jit(solution)/shard_map/ppermute | solution.py:12
  59.7 0.4 fusion.44
  60.5 64.8 %collective-permute-start.7 = (bf16[256,1152]{1,0:T(8,128)(2,1)S(1)}, bf16[256,1152]{1,0:T(8,128)(2,1)S(1)}, u32[]{:S(2)}, u32[]{:S(2)}) collective-permute-start(bf16[256,1152]{1,0:T(8,128)(2,1)S(1)} %convolution_convert_fusion), channel_id=1, source_target_pairs={{0,736},{32,0},{64,32},{96,64},{128,96},{160,128},{192,160},{224,1... | collective-permute-start | bytes 1769480 | tf_op jit(solution)/shard_map/ppermute | solution.py:12
  125.3 0.4 fusion.41
  126.1 1.9 collective-permute-start.5
  128.0 0.4 fusion.43
  128.8 52.8 %collective-permute-start.8 = (bf16[256,1152]{1,0:T(8,128)(2,1)S(1)}, bf16[256,1152]{1,0:T(8,128)(2,1)S(1)}, u32[]{:S(2)}, u32[]{:S(2)}) collective-permute-start(bf16[256,1152]{1,0:T(8,128)(2,1)S(1)} %add_convert_fusion.2), channel_id=1, source_target_pairs={{0,736},{32,0},{64,32},{96,64},{128,96},{160,128},{192,160},{224,1... | collective-permute-start | bytes 1769480 | tf_op jit(solution)/shard_map/ppermute | solution.py:12
  181.6 0.4 fusion.40
  182.4 0.4 add_convert_fusion.3
  182.7 9.8 %collective-permute-start.6 = (bf16[256,1152]{1,0:T(8,128)(2,1)S(1)}, bf16[256,1152]{1,0:T(8,128)(2,1)S(1)}, u32[]{:S(2)}, u32[]{:S(2)}) collective-permute-start(bf16[256,1152]{1,0:T(8,128)(2,1)S(1)} %add_convert_fusion.3), channel_id=1, source_target_pairs={{0,736},{32,0},{64,32},{96,64},{128,96},{160,128},{192,160},{224,1... | collective-permute-start | bytes 1769480 | tf_op jit(solution)/shard_map/ppermute | solution.py:12
  192.7 1.9 collective-permute-start.9
  195.3 1.2 fusion.1
  196.5 43.1 %collective-permute-done.9 = bf16[256,1152]{1,0:T(8,128)(2,1)S(1)} collective-permute-done((bf16[256,1152]{1,0:T(8,128)(2,1)S(1)}, bf16[256,1152]{1,0:T(8,128)(2,1)S(1)}, u32[]{:S(2)}, u32[]{:S(2)}) %collective-permute-start.9) | collective-permute-done | bytes 589856 | tf_op jit(solution)/shard_map/ppermute | solution.py:12
  239.6 1.0 add_convert_fusion
  (20 shorter events, 3.3 us)
Async XLA Ops:
  0.6 21.0 %copy-start = (bf16[256,1152]{1,0:T(8,128)(2,1)S(1)}, bf16[256,1152]{1,0:T(8,128)(2,1)}, u32[]{:S(2)}) copy-start(bf16[256,1152]{1,0:T(8,128)(2,1)} %param.5) | copy-start | bytes 1769476
  0.6 16.4 %collective-permute-start.2 = (bf16[256,1152]{1,0:T(8,128)(2,1)}, bf16[256,1152]{1,0:T(8,128)(2,1)S(1)}, u32[]{:S(2)}, u32[]{:S(2)}) collective-permute-start(bf16[256,1152]{1,0:T(8,128)(2,1)} %param.6), channel_id=1, source_target_pairs={{0,1},{1,2},{2,3},{3,4},{4,5},{5,6},{6,7},{7,8},{8,9},{9,10},{10,1... | collective-permute-start | bytes 1769480 | tf_op jit(solution)/shard_map/ppermute | solution.py:12
  3.9 20.0 %collective-permute-start = (bf16[256,1152]{1,0:T(8,128)(2,1)}, bf16[256,1152]{1,0:T(8,128)(2,1)S(1)}, u32[]{:S(2)}, u32[]{:S(2)}) collective-permute-start(bf16[256,1152]{1,0:T(8,128)(2,1)} %param.6), channel_id=1, source_target_pairs={{0,32},{32,64},{64,96},{96,128},{128,160},{160,192},{192,224},{224... | collective-permute-start | bytes 1769480 | tf_op jit(solution)/shard_map/ppermute | solution.py:12
  17.1 11.4 %collective-permute-start.3 = (bf16[256,1152]{1,0:T(8,128)(2,1)S(1)}, bf16[256,1152]{1,0:T(8,128)(2,1)S(1)}, u32[]{:S(2)}, u32[]{:S(2)}) collective-permute-start(bf16[256,1152]{1,0:T(8,128)(2,1)S(1)} %collective-permute-done.2), channel_id=1, source_target_pairs={{0,32},{32,64},{64,96},{96,128},{128,160},{160,192},{192,224},{224... | collective-permute-start | bytes 1769480 | tf_op jit(solution)/shard_map/ppermute | solution.py:12
  21.6 1.6 copy-start.1
  23.9 101.4 %collective-permute-start.1 = (bf16[256,1152]{1,0:T(8,128)(2,1)S(1)}, bf16[256,1152]{1,0:T(8,128)(2,1)S(1)}, u32[]{:S(2)}, u32[]{:S(2)}) collective-permute-start(bf16[256,1152]{1,0:T(8,128)(2,1)S(1)} %collective-permute-done), channel_id=1, source_target_pairs={{0,32},{32,64},{64,96},{96,128},{128,160},{160,192},{192,224},{224... | collective-permute-start | bytes 1769480 | tf_op jit(solution)/shard_map/ppermute | solution.py:12
  28.4 31.3 %collective-permute-start.4 = (bf16[256,1152]{1,0:T(8,128)(2,1)S(1)}, bf16[256,1152]{1,0:T(8,128)(2,1)S(1)}, u32[]{:S(2)}, u32[]{:S(2)}) collective-permute-start(bf16[256,1152]{1,0:T(8,128)(2,1)S(1)} %collective-permute-done.3), channel_id=1, source_target_pairs={{0,32},{32,64},{64,96},{96,128},{128,160},{160,192},{192,224},{224... | collective-permute-start | bytes 1769480 | tf_op jit(solution)/shard_map/ppermute | solution.py:12
  60.5 67.9 %collective-permute-start.7 = (bf16[256,1152]{1,0:T(8,128)(2,1)S(1)}, bf16[256,1152]{1,0:T(8,128)(2,1)S(1)}, u32[]{:S(2)}, u32[]{:S(2)}) collective-permute-start(bf16[256,1152]{1,0:T(8,128)(2,1)S(1)} %convolution_convert_fusion), channel_id=1, source_target_pairs={{0,736},{32,0},{64,32},{96,64},{128,96},{160,128},{192,160},{224,1... | collective-permute-start | bytes 1769480 | tf_op jit(solution)/shard_map/ppermute | solution.py:12
  126.1 56.3 %collective-permute-start.5 = (bf16[256,1152]{1,0:T(8,128)(2,1)S(1)}, bf16[256,1152]{1,0:T(8,128)(2,1)S(1)}, u32[]{:S(2)}, u32[]{:S(2)}) collective-permute-start(bf16[256,1152]{1,0:T(8,128)(2,1)S(1)} %convolution_convert_fusion.1), channel_id=1, source_target_pairs={{0,736},{32,0},{64,32},{96,64},{128,96},{160,128},{192,160},{224,1... | collective-permute-start | bytes 1769480 | tf_op jit(solution)/shard_map/ppermute | solution.py:12
  128.8 63.8 %collective-permute-start.8 = (bf16[256,1152]{1,0:T(8,128)(2,1)S(1)}, bf16[256,1152]{1,0:T(8,128)(2,1)S(1)}, u32[]{:S(2)}, u32[]{:S(2)}) collective-permute-start(bf16[256,1152]{1,0:T(8,128)(2,1)S(1)} %add_convert_fusion.2), channel_id=1, source_target_pairs={{0,736},{32,0},{64,32},{96,64},{128,96},{160,128},{192,160},{224,1... | collective-permute-start | bytes 1769480 | tf_op jit(solution)/shard_map/ppermute | solution.py:12
  182.7 13.8 %collective-permute-start.6 = (bf16[256,1152]{1,0:T(8,128)(2,1)S(1)}, bf16[256,1152]{1,0:T(8,128)(2,1)S(1)}, u32[]{:S(2)}, u32[]{:S(2)}) collective-permute-start(bf16[256,1152]{1,0:T(8,128)(2,1)S(1)} %add_convert_fusion.3), channel_id=1, source_target_pairs={{0,736},{32,0},{64,32},{96,64},{128,96},{160,128},{192,160},{224,1... | collective-permute-start | bytes 1769480 | tf_op jit(solution)/shard_map/ppermute | solution.py:12
  192.7 46.9 %collective-permute-start.9 = (bf16[256,1152]{1,0:T(8,128)(2,1)S(1)}, bf16[256,1152]{1,0:T(8,128)(2,1)S(1)}, u32[]{:S(2)}, u32[]{:S(2)}) collective-permute-start(bf16[256,1152]{1,0:T(8,128)(2,1)S(1)} %add_convert_fusion.1), channel_id=1, source_target_pairs={{0,31},{1,0},{2,1},{3,2},{4,3},{5,4},{6,5},{7,6},{8,7},{9,8},{10,9... | collective-permute-start | bytes 1769480 | tf_op jit(solution)/shard_map/ppermute | solution.py:12
where the time goes:
time: 241 us
  starting transfers between devices  149 us (62%)
  waiting for transfers between devices  78.8 us (33%)
  matrix products  8.62 us (4%)
  between operations  2.82 us (1%)
    ppermute x10, starting transfers between devices, from_behind(): return lax.ppermute(value, axis, pairs)  149 us
    ppermute x10, waiting for transfers between devices, from_behind(): return lax.ppermute(value, axis, pairs)  78.8 us
  transfers between devices with their start and end apart: 10, of which 4 were waited for; matrix products, arithmetic and copies ran while one was open for 4% of the time, Pallas kernels for 0%

commit v1 on v0

v1 whole, which is shorter than its diff:
```python
import functools

import jax
import jax.numpy as jnp
from jax import lax
from jax.experimental import pallas as pl
from jax.experimental.pallas import tpu as pltpu
from jax.sharding import PartitionSpec as P

MESH = pl.DeviceIdType.MESH
ROWS = 256
D = 1152
PIECE = 64
PAIRS = 196608
N_X, N_Y, N_HI, N_LO = 4, 8, 3, 4


def device(hi, x, core, y, lo):
    return ((hi * N_X + x) * 2 + core, y * N_LO + lo)


def kernel(
    sharp_ref,
    shift_ref,
    adj_ref,
    img_ref,
    txt_ref,
    gimg_ref,
    gtxt_ref,
    texts,
    images,
    weights,
    hop_img,
    hop_grad,
    sib_out,
    sib_in,
    next_out,
    next_in,
    text_out,
    text_in,
    load_sem,
    send_sem,
    recv_sem,
):
    blk = lax.axis_index("blk")
    grp = lax.axis_index("grp")
    core = lax.rem(blk, 2)
    x = lax.rem(lax.div(blk, 2), N_X)
    hi = lax.div(blk, 2 * N_X)
    grp_next = (blk, lax.rem(grp + 1, N_Y * N_LO))
    grp_prev = (blk, lax.rem(grp + N_Y * N_LO - 1, N_Y * N_LO))
    sibling = (blk + 1 - 2 * core, grp)
    hi_up = lax.rem(hi + 1, N_HI)
    hi_down = lax.rem(hi + N_HI - 1, N_HI)

    def line(which, at_hi):
        return ((at_hi * N_X + which) * 2 + core, grp)

    load_i = pltpu.make_async_copy(img_ref, images.at[pl.ds(0, ROWS)], load_sem.at[0])
    load_t = pltpu.make_async_copy(txt_ref, texts.at[pl.ds(0, ROWS)], load_sem.at[1])
    load_i.start()
    load_t.start()

    barrier = pltpu.get_barrier_semaphore()

    def greet(target):
        pl.semaphore_signal(barrier, inc=1, device_id=target, device_id_type=MESH)

    greet(grp_next)
    greet(grp_prev)
    greet(sibling)
    for step in range(1, N_X):
        greet(line(lax.rem(x + step, N_X), hi))

    @pl.when(x == N_X - 1)
    def _():
        for which in range(N_X):
            greet(line(which, hi_up))

    @pl.when(x == 0)
    def _():
        for which in range(N_X):
            greet(line(which, hi_down))

    sharp = sharp_ref[0]
    shift = shift_ref[0]
    scale = adj_ref[0] * sharp / PAIRS

    def make_weights(image, text):
        logits = lax.dot_general(
            images[pl.ds(image * ROWS, ROWS), :],
            texts[pl.ds(text * ROWS, ROWS), :],
            (((1,), (1,)), ((), ())),
            preferred_element_type=jnp.float32,
        )
        likely = jax.nn.sigmoid(sharp * logits + shift)
        if image == 0 and text == 0:
            cols = lax.broadcasted_iota(jnp.int32, likely.shape, 1)
            rows = lax.broadcasted_iota(jnp.int32, likely.shape, 0)
            likely = likely - (cols == rows).astype(jnp.float32)
        weights[pl.ds(image * ROWS, ROWS), pl.ds(text * ROWS, ROWS)] = (
            scale * likely
        ).astype(jnp.bfloat16)

    def image_grad(image):
        return jnp.dot(
            weights[pl.ds(image * ROWS, ROWS), :],
            texts[...],
            preferred_element_type=jnp.float32,
        )

    def text_grad(text):
        return lax.dot_general(
            weights[:, pl.ds(text * ROWS, ROWS)],
            images[...],
            (((0,), (0,)), ((), ())),
            preferred_element_type=jnp.float32,
        )

    def send(src, dst, which, arrival, target):
        return pltpu.make_async_remote_copy(
            src_ref=src,
            dst_ref=dst,
            send_sem=send_sem.at[which],
            recv_sem=recv_sem.at[arrival],
            device_id=target,
            device_id_type=MESH,
        )

    own_i = images.at[pl.ds(0, ROWS)]
    got_s = images.at[pl.ds(ROWS, ROWS)]
    got_x = images.at[pl.ds(2 * ROWS, ROWS)]

    def piece(ref, which, base=0):
        return ref.at[pl.ds(base + which * PIECE, PIECE)]

    load_i.wait()
    load_t.wait()
    make_weights(0, 0)
    pl.semaphore_wait(barrier, 8)

    send_text = send(texts.at[pl.ds(0, ROWS)], texts.at[pl.ds(ROWS, ROWS)], 0, 0, grp_next)
    send_text.start()
    send_image = send(own_i, got_x, 1, 1, line(lax.rem(x + N_X - 1, N_X), hi))
    send_first = send(
        piece(images, 0), piece(images, 0, 2 * ROWS), 1, 1, line(N_X - 1, hi_down)
    )
    to_relay = [
        send(piece(images, q), hop_img, 1 + q, 3, line(q, hi)) for q in range(1, N_X)
    ]
    relay_image = send(
        hop_img, piece(images, x, 2 * ROWS), 5, 1, line(N_X - 1, hi_down)
    )
    send_sib = send(own_i, got_s, 6, 2, sibling)
    forward_sib = send(got_x, got_s, 6, 2, sibling)

    @pl.when(x > 0)
    def _():
        send_image.start()

    @pl.when(x == 0)
    def _():
        for copy in to_relay:
            copy.start()
        send_first.start()

    @pl.when(core == 1)
    def _():
        send_sib.start()

    @pl.when(x > 0)
    def _():
        send(hop_img, hop_img, 1, 3, sibling).wait_recv()
        relay_image.start()

    wait_x = send(got_x, got_x, 1, 1, sibling)

    @pl.when(core == 0)
    def _():
        wait_x.wait_recv()
        forward_sib.start()

    send_text.wait_recv()
    make_weights(0, 1)

    send_sib.wait_recv()
    make_weights(1, 0)
    make_weights(1, 1)
    sib_out[...] = image_grad(1).astype(jnp.bfloat16)
    return_sib = send(sib_out, sib_in, 7, 4, sibling)
    return_sib.start()

    @pl.when(core == 1)
    def _():
        wait_x.wait_recv()

    make_weights(2, 0)
    make_weights(2, 1)
    grad_x = image_grad(2)

    @pl.when(core == 0)
    def _():
        return_sib.wait_recv()
        next_out[...] = (grad_x + sib_in[...].astype(jnp.float32)).astype(jnp.bfloat16)

    @pl.when(core == 1)
    def _():
        next_out[...] = grad_x.astype(jnp.bfloat16)

    send_grad = send(next_out, next_in, 8, 5, line(lax.rem(x + 1, N_X), hi))
    send_last = send(
        piece(next_out, N_X - 1), piece(next_in, N_X - 1), 8, 5, line(0, hi_up)
    )
    grad_to_relay = [
        send(piece(next_out, q), hop_grad, 9 + q, 7, line(q, hi)) for q in range(N_X - 1)
    ]
    relay_grad = send(hop_grad, piece(next_in, x), 12, 5, line(0, hi_up))

    @pl.when(x < N_X - 1)
    def _():
        send_grad.start()

    @pl.when(x == N_X - 1)
    def _():
        for copy in grad_to_relay:
            copy.start()
        send_last.start()

    text_out[...] = text_grad(1).astype(jnp.bfloat16)
    return_text = send(text_out, text_in, 13, 6, grp_prev)
    return_text.start()

    @pl.when(x < N_X - 1)
    def _():
        send(hop_grad, hop_grad, 12, 7, sibling).wait_recv()
        relay_grad.start()

    grad_t = text_grad(0)
    grad_i = image_grad(0)

    @pl.when(core == 1)
    def _():
        return_sib.wait_recv()

    send_grad.wait_recv()

    @pl.when(core == 0)
    def _():
        gimg_ref[...] = (grad_i + next_in[...].astype(jnp.float32)).astype(jnp.bfloat16)

    @pl.when(core == 1)
    def _():
        gimg_ref[...] = (
            grad_i
            + next_in[...].astype(jnp.float32)
            + sib_in[...].astype(jnp.float32)
        ).astype(jnp.bfloat16)

    return_text.wait_recv()
    gtxt_ref[...] = (grad_t + text_in[...].astype(jnp.float32)).astype(jnp.bfloat16)

    send_text.wait_send()

    @pl.when(x > 0)
    def _():
        send_image.wait_send()
        relay_image.wait_send()

    @pl.when(x == 0)
    def _():
        send_first.wait_send()
        for copy in to_relay:
            copy.wait_send()

    send_sib.wait_send()
    return_sib.wait_send()

    @pl.when(x < N_X - 1)
    def _():
        send_grad.wait_send()
        relay_grad.wait_send()

    @pl.when(x == N_X - 1)
    def _():
        send_last.wait_send()
        for copy in grad_to_relay:
            copy.wait_send()

    return_text.wait_send()


def on_device(img, txt, sharp, shift, adj):
    shard = jax.ShapeDtypeStruct((ROWS, D), jnp.bfloat16)

    def half(rows, cols=D):
        return pltpu.VMEM((rows, cols), jnp.bfloat16)

    return pl.pallas_call(
        kernel,
        out_shape=(shard, shard),
        in_specs=[pl.BlockSpec(memory_space=pltpu.SMEM)] * 3
        + [pl.BlockSpec(memory_space=pl.ANY)] * 2,
        out_specs=[pl.BlockSpec(memory_space=pltpu.VMEM)] * 2,
        scratch_shapes=[
            half(2 * ROWS),
            half(3 * ROWS),
            half(3 * ROWS, 2 * ROWS),
            half(PIECE),
            half(PIECE),
            half(ROWS),
            half(ROWS),
            half(ROWS),
            half(ROWS),
            half(ROWS),
            half(ROWS),
            pltpu.SemaphoreType.DMA((2,)),
            pltpu.SemaphoreType.DMA((14,)),
            pltpu.SemaphoreType.DMA((8,)),
        ],
        compiler_params=pltpu.CompilerParams(
            collective_id=0, has_side_effects=True, vmem_limit_bytes=48 << 20
        ),
        cost_estimate=pl.CostEstimate(
            flops=18 * 2 * ROWS * ROWS * D, bytes_accessed=4 * ROWS * D * 2, transcendentals=6 * ROWS * ROWS
        ),
    )(sharp, shift, adj, img, txt)


def solution(mesh):
    return jax.shard_map(
        on_device,
        mesh=mesh,
        in_specs=(P(("blk", "grp"), None), P(("blk", "grp"), None), P(), P(), P()),
        out_specs=(P(("blk", "grp"), None), P(("blk", "grp"), None)),
        check_vma=False,
    )
```

time: 241 us -> 81.2 us (0.34)
  the two profiles are of different devices: /device:TPU:577 before, /device:TPU:129 now
where the time goes in v1:
time: 81.2 us; the launch traced here: 80.9 us
  Pallas kernels  74.6 us (92%)
  local copies, waits for them, and re-layouts  3.75 us (5%)
  between operations  2.58 us (3%)
    pallas_call x1, Pallas kernels, on_device(): pl.pallas_call(kernel, out_shape=(shard, shard), in_specs=[pl.BlockSpec(m...  74.6 us
    unnamed x6, local copies, waits for them, and re-layouts  3.75 us

profile of v1, /device:TPU:129, one launch (start us, length us, event | category | flops | bytes accessed | tf_op | source)
XLA Modules:
  0.0 80.9 jit_solution(16942379137157557056)
XLA Ops:
  2.6 0.0 copy-start
  2.6 1.1 %copy-done = bf16[256,1152]{1,0:T(8,128)(2,1)S(1)} copy-done((bf16[256,1152]{1,0:T(8,128)(2,1)S(1)}, bf16[256,1152]{1,0:T(8,128)(2,1)}, u32[]{:S(2)}) %copy-start) | copy-done | bytes 589848
  3.6 0.0 copy-start.1
  3.6 1.1 %copy-done.1 = bf16[256,1152]{1,0:T(8,128)(2,1)S(1)} copy-done((bf16[256,1152]{1,0:T(8,128)(2,1)S(1)}, bf16[256,1152]{1,0:T(8,128)(2,1)}, u32[]{:S(2)}) %copy-start.1) | copy-done | bytes 589848
  4.7 74.6 %shard_map.68 = (bf16[256,1152]{1,0:T(8,128)(2,1)S(1)}, bf16[256,1152]{1,0:T(8,128)(2,1)S(1)}) custom-call(f32[1]{0:T(128)S(6)} %copy.9.sharp_ref, f32[1]{0:T(128)S(6)} %copy.10.shift_ref, f32[1]{0:T(128)S(6)} %copy.11.adj_ref, bf16[256,1152]{1,0:T(8,128)(2,1)S(1)} %copy-done, bf16[256,1152]{1,0:T(8,128)(2,1)S(1)} %copy-done.1), custom_call_target="tpu_custom_call" | custom-call | flops 2717908992 | bytes 2359296 | tf_op jit(solution)/shard_map/pallas_call | solution.py:298
  79.3 0.8 %copy.12 = bf16[256,1152]{1,0:T(8,128)(2,1)} copy(bf16[256,1152]{1,0:T(8,128)(2,1)S(1)} %get-tuple-element.4) | data formatting | bytes 1179648
  80.1 0.8 %copy.13 = bf16[256,1152]{1,0:T(8,128)(2,1)} copy(bf16[256,1152]{1,0:T(8,128)(2,1)S(1)} %get-tuple-element.5) | data formatting | bytes 1179648
Async XLA Ops:
  2.6 1.1 %copy-start = (bf16[256,1152]{1,0:T(8,128)(2,1)S(1)}, bf16[256,1152]{1,0:T(8,128)(2,1)}, u32[]{:S(2)}) copy-start(bf16[256,1152]{1,0:T(8,128)(2,1)} %img_ref.1) | copy-start | bytes 1769476
  3.6 1.1 %copy-start.1 = (bf16[256,1152]{1,0:T(8,128)(2,1)S(1)}, bf16[256,1152]{1,0:T(8,128)(2,1)}, u32[]{:S(2)}) copy-start(bf16[256,1152]{1,0:T(8,128)(2,1)} %txt_ref.1) | copy-start | bytes 1769476

commit v2 on v1

v2 whole, which is shorter than its diff:
```python
import functools

import jax
import jax.numpy as jnp
from jax import lax
from jax.experimental import pallas as pl
from jax.experimental.pallas import tpu as pltpu
from jax.sharding import PartitionSpec as P

MESH = pl.DeviceIdType.MESH
ROWS = 256
D = 1152
HALF = 128
PIECE = 32
PAIRS = 196608
N_X, N_Y, N_HI, N_LO = 4, 8, 3, 4


def device(hi, x, core, y, lo):
    return ((hi * N_X + x) * 2 + core, y * N_LO + lo)


def kernel(
    sharp_ref,
    shift_ref,
    adj_ref,
    img_ref,
    txt_ref,
    gimg_ref,
    gtxt_ref,
    texts,
    images,
    weights,
    hop_img,
    hop_grad,
    next_out,
    next_in,
    part_out,
    part_in,
    text_out,
    text_in,
    load_sem,
    send_sem,
    recv_sem,
    far_sem,
):
    blk = lax.axis_index("blk")
    grp = lax.axis_index("grp")
    core = lax.rem(blk, 2)
    x = lax.rem(lax.div(blk, 2), N_X)
    hi = lax.div(blk, 2 * N_X)
    grp_lo = lax.rem(grp, N_LO)
    grp_next = (blk, lax.rem(grp + 1, N_Y * N_LO))
    grp_prev = (blk, lax.rem(grp + N_Y * N_LO - 1, N_Y * N_LO))
    sibling = (blk + 1 - 2 * core, grp)
    hi_up = lax.rem(hi + 1, N_HI)
    hi_down = lax.rem(hi + N_HI - 1, N_HI)

    def line(which, at_hi):
        return ((at_hi * N_X + which) * 2 + core, grp)

    own_t, near_t, sib_t, sib_near_t = (
        texts.at[pl.ds(ROWS * n, ROWS)] for n in range(4)
    )
    own_i = images.at[pl.ds(0, ROWS)]

    load_i = pltpu.make_async_copy(img_ref, own_i, load_sem.at[0])
    load_t = pltpu.make_async_copy(txt_ref, own_t, load_sem.at[1])
    load_i.start()
    load_t.start()

    barrier = pltpu.get_barrier_semaphore()

    def greet(target):
        pl.semaphore_signal(barrier, inc=1, device_id=target, device_id_type=MESH)

    greet(grp_prev)
    greet(sibling)

    @pl.when(x == 0)
    def _():
        greet(line(1, hi))

    @pl.when(x > 0)
    def _():
        greet(line(0, hi))

    @pl.when(x == 1)
    def _():
        greet(line(2, hi))

    @pl.when(x < N_X - 1)
    def _():
        greet(line(N_X - 1, hi))

    wraps = hi == 0

    @pl.when((x == N_X - 1) & (hi < N_HI - 1))
    def _():
        for which in range(N_X):
            greet(line(which, hi_up))

    @pl.when(wraps)
    def _():
        greet(line(N_X - 1, hi_down))

    sharp = sharp_ref[0]
    shift = shift_ref[0]
    scale = adj_ref[0] * sharp / PAIRS

    def make_weights(row, rows, text, own_pair=False):
        logits = lax.dot_general(
            images[pl.ds(row, rows), :],
            texts[pl.ds(text * ROWS, ROWS), :],
            (((1,), (1,)), ((), ())),
            preferred_element_type=jnp.float32,
        )
        likely = jax.nn.sigmoid(sharp * logits + shift)
        if own_pair:
            cols = lax.broadcasted_iota(jnp.int32, likely.shape, 1)
            at_row = lax.broadcasted_iota(jnp.int32, likely.shape, 0)
            likely = likely - (cols == at_row).astype(jnp.float32)
        weights[pl.ds(row, rows), pl.ds(text * ROWS, ROWS)] = (scale * likely).astype(
            jnp.bfloat16
        )

    def image_grad(row, rows, n_texts):
        return jnp.dot(
            weights[pl.ds(row, rows), pl.ds(0, n_texts * ROWS)],
            texts[pl.ds(0, n_texts * ROWS), :],
            preferred_element_type=jnp.float32,
        )

    def text_grad(row, rows, text):
        return lax.dot_general(
            weights[pl.ds(row, rows), pl.ds(text * ROWS, ROWS)],
            images[pl.ds(row, rows), :],
            (((0,), (0,)), ((), ())),
            preferred_element_type=jnp.float32,
        )

    def send(src, dst, which, arrival, target):
        return pltpu.make_async_remote_copy(
            src_ref=src,
            dst_ref=dst,
            send_sem=send_sem.at[which],
            recv_sem=recv_sem.at[arrival],
            device_id=target,
            device_id_type=MESH,
        )

    def arrived(ref, arrival):
        send(ref, ref, 0, arrival, sibling).wait_recv()

    def half(ref, h, base=0):
        return ref.at[pl.ds(base + h * HALF, HALF)]

    def piece(ref, h, q, base=0):
        return ref.at[pl.ds(base + h * HALF + q * PIECE, PIECE)]

    up_line = line(0, hi_up)
    down_line = line(N_X - 1, hi_down)
    x_up = line(lax.rem(x + 1, N_X), hi)
    x_down = line(lax.rem(x + N_X - 1, N_X), hi)

    send_text = send(own_t, near_t, 0, 0, grp_next)
    share_text = send(own_t, sib_t, 1, 1, sibling)
    share_near = send(near_t, sib_near_t, 2, 2, sibling)
    image_direct, image_first, image_spread, image_relay = [], [], [], []
    grad_direct, grad_last, grad_spread, grad_relay = [], [], [], []
    for h in range(2):
        image_direct.append(
            send(half(images, h), half(images, h, ROWS), 3 + h, 3 + h, x_down)
        )
        image_first.append(
            send(piece(images, h, 0), piece(images, h, 0, ROWS), 3 + h, 3 + h, down_line)
        )
        image_spread.append(
            [
                send(piece(images, h, q), hop_img.at[h], 5 + 3 * h + q, 5 + h, line(q, hi))
                for q in range(1, N_X)
            ]
        )
        image_relay.append(
            send(hop_img.at[h], piece(images, h, x, ROWS), 12 + h, 3 + h, down_line)
        )
        grad_direct.append(send(half(next_out, h), half(next_in, h), 14 + h, 7 + h, x_up))
        grad_last.append(
            send(
                piece(next_out, h, N_X - 1),
                piece(next_in, h, N_X - 1),
                14 + h,
                7 + h,
                up_line,
            )
        )
        grad_spread.append(
            [
                send(piece(next_out, h, q), hop_grad.at[h], 16 + 3 * h + q, 9 + h, line(q, hi))
                for q in range(N_X - 1)
            ]
        )
        grad_relay.append(
            send(hop_grad.at[h], piece(next_in, h, x), 22 + h, 7 + h, up_line)
        )
    share_part = [send(part_out.at[t], part_in.at[t], 24 + t, 11 + t, sibling) for t in range(2)]
    return_text = send(text_out, text_in, 26, 13, grp_prev)

    load_i.wait()
    load_t.wait()
    make_weights(0, ROWS, 0, own_pair=True)
    first = jnp.where((x == 0) | (x == N_X - 1), 5, 3)
    first = first + jnp.where(hi > 0, 1, 0)
    first = first + jnp.where((x == N_X - 1) & (hi == N_HI - 1), N_X, 0)
    pl.semaphore_wait(barrier, first)

    @pl.when((x == N_X - 1) & (hi == N_HI - 1))
    def _():
        for which in range(N_X):
            pl.semaphore_signal(
                far_sem, inc=1, device_id=line(which, hi_up), device_id_type=MESH
            )

    def await_far():
        @pl.when(wraps)
        def _():
            pl.semaphore_wait(far_sem, 1)

    @pl.when(x == 0)
    def _():
        for h in range(2):
            for copy in image_spread[h]:
                copy.start()

    @pl.when(x > 0)
    def _():
        for h in range(2):
            image_direct[h].start()

    send_text.start()
    share_text.start()

    await_far()

    @pl.when(x == 0)
    def _():
        for h in (0,):
            image_first[h].start()

    @pl.when(x > 0)
    def _():
        for h in (0,):
            arrived(hop_img.at[h], 5 + h)
            image_relay[h].start()

    share_text.wait_recv()

    @pl.when(core == 1)
    def _():
        make_weights(0, ROWS, 2)

    send_text.wait_recv()
    share_near.start()
    @pl.when(x == 0)
    def _():
        for h in (1,):
            image_first[h].start()

    @pl.when(x > 0)
    def _():
        for h in (1,):
            arrived(hop_img.at[h], 5 + h)
            image_relay[h].start()


    make_weights(0, ROWS, 1)
    share_near.wait_recv()

    @pl.when(core == 1)
    def _():
        make_weights(0, ROWS, 3)

    for h in range(2):
        arrived(half(images, h, ROWS), 3 + h)
        row = ROWS + h * HALF
        make_weights(row, HALF, 0)
        make_weights(row, HALF, 1)

        @pl.when(core == 0)
        def _():
            make_weights(row, HALF, 2)
            make_weights(row, HALF, 3)
            half(next_out, h)[...] = image_grad(row, HALF, 4).astype(jnp.bfloat16)

        @pl.when(core == 1)
        def _():
            half(next_out, h)[...] = image_grad(row, HALF, 2).astype(jnp.bfloat16)

        @pl.when(x < N_X - 1)
        def _():
            grad_direct[h].start()

        @pl.when(x == N_X - 1)
        def _():
            for copy in grad_spread[h]:
                copy.start()
            grad_last[h].start()

    both = pl.multiple_of((1 - core) * ROWS, ROWS)
    for t in (1, 0):
        part_out[t] = text_grad(both, ROWS, 2 + t).astype(jnp.bfloat16)
        share_part[t].start()
    grad_near = text_grad(0, 2 * ROWS, 1)
    share_part[1].wait_recv()
    text_out[...] = (grad_near + part_in[1].astype(jnp.float32)).astype(jnp.bfloat16)

    @pl.when(x == 0)
    def _():
        image_first[1].wait_send()

    @pl.when(x > 0)
    def _():
        image_relay[1].wait_send()

    @pl.when(grp_lo > 0)
    def _():
        return_text.start()

    @pl.when(x < N_X - 1)
    def _():
        for h in range(2):
            arrived(hop_grad.at[h], 9 + h)
            grad_relay[h].start()

    @pl.when(grp_lo == 0)
    def _():
        return_text.start()

    grad_t = text_grad(0, 2 * ROWS, 0)
    share_part[0].wait_recv()
    grad_t = grad_t + part_in[0].astype(jnp.float32)

    for h in range(2):
        arrived(half(next_in, h), 7 + h)

    @pl.when(core == 0)
    def _():
        gimg_ref[...] = (
            image_grad(0, ROWS, 2) + next_in[...].astype(jnp.float32)
        ).astype(jnp.bfloat16)

    @pl.when(core == 1)
    def _():
        gimg_ref[...] = (
            image_grad(0, ROWS, 4) + next_in[...].astype(jnp.float32)
        ).astype(jnp.bfloat16)

    return_text.wait_recv()
    gtxt_ref[...] = (grad_t + text_in[...].astype(jnp.float32)).astype(jnp.bfloat16)

    for copy in [send_text, share_text, share_near, return_text] + share_part:
        copy.wait_send()

    @pl.when(x == 0)
    def _():
        image_first[0].wait_send()
        for h in range(2):
            for copy in image_spread[h]:
                copy.wait_send()

    @pl.when(x > 0)
    def _():
        for h in range(2):
            image_direct[h].wait_send()
        image_relay[0].wait_send()

    @pl.when(x < N_X - 1)
    def _():
        for h in range(2):
            grad_direct[h].wait_send()
            grad_relay[h].wait_send()

    @pl.when(x == N_X - 1)
    def _():
        for h in range(2):
            grad_last[h].wait_send()
            for copy in grad_spread[h]:
                copy.wait_send()


def on_device(img, txt, sharp, shift, adj):
    shard = jax.ShapeDtypeStruct((ROWS, D), jnp.bfloat16)

    def half(rows, cols=D):
        return pltpu.VMEM((rows, cols), jnp.bfloat16)

    return pl.pallas_call(
        kernel,
        out_shape=(shard, shard),
        in_specs=[pl.BlockSpec(memory_space=pltpu.SMEM)] * 3
        + [pl.BlockSpec(memory_space=pl.ANY)] * 2,
        out_specs=[pl.BlockSpec(memory_space=pltpu.VMEM)] * 2,
        scratch_shapes=[
            half(4 * ROWS),
            half(2 * ROWS),
            half(2 * ROWS, 4 * ROWS),
            pltpu.VMEM((2, PIECE, D), jnp.bfloat16),
            pltpu.VMEM((2, PIECE, D), jnp.bfloat16),
            half(ROWS),
            half(ROWS),
            pltpu.VMEM((2, ROWS, D), jnp.bfloat16),
            pltpu.VMEM((2, ROWS, D), jnp.bfloat16),
            half(ROWS),
            half(ROWS),
            pltpu.SemaphoreType.DMA((2,)),
            pltpu.SemaphoreType.DMA((27,)),
            pltpu.SemaphoreType.DMA((14,)),
            pltpu.SemaphoreType.REGULAR,
        ],
        compiler_params=pltpu.CompilerParams(
            collective_id=0, has_side_effects=True, vmem_limit_bytes=48 << 20
        ),
        cost_estimate=pl.CostEstimate(
            flops=18 * 2 * ROWS * ROWS * D, bytes_accessed=4 * ROWS * D * 2, transcendentals=6 * ROWS * ROWS
        ),
    )(sharp, shift, adj, img, txt)


def solution(mesh):
    return jax.shard_map(
        on_device,
        mesh=mesh,
        in_specs=(P(("blk", "grp"), None), P(("blk", "grp"), None), P(), P(), P()),
        out_specs=(P(("blk", "grp"), None), P(("blk", "grp"), None)),
        check_vma=False,
    )
```

time: 81.2 us -> 73 us (0.90)
  the two profiles are of different devices: /device:TPU:129 before, /device:TPU:1 now
where the time goes in v2:
time: 73 us; the launch traced here: 72.7 us
  Pallas kernels  66.4 us (91%)
  local copies, waits for them, and re-layouts  3.75 us (5%)
  between operations  2.58 us (4%)
    pallas_call x1, Pallas kernels, on_device(): pl.pallas_call(kernel, out_shape=(shard, shard), in_specs=[pl.BlockSpec(m...  66.4 us
    unnamed x6, local copies, waits for them, and re-layouts  3.75 us

profile of v2, /device:TPU:1, one launch (start us, length us, event | category | flops | bytes accessed | tf_op | source)
XLA Modules:
  0.0 72.7 jit_solution(5665605730566319480)
XLA Ops:
  2.6 0.0 copy-start
  2.6 1.1 %copy-done = bf16[256,1152]{1,0:T(8,128)(2,1)S(1)} copy-done((bf16[256,1152]{1,0:T(8,128)(2,1)S(1)}, bf16[256,1152]{1,0:T(8,128)(2,1)}, u32[]{:S(2)}) %copy-start) | copy-done | bytes 589848
  3.6 0.0 copy-start.1
  3.6 1.1 %copy-done.1 = bf16[256,1152]{1,0:T(8,128)(2,1)S(1)} copy-done((bf16[256,1152]{1,0:T(8,128)(2,1)S(1)}, bf16[256,1152]{1,0:T(8,128)(2,1)}, u32[]{:S(2)}) %copy-start.1) | copy-done | bytes 589848
  4.7 66.4 %shard_map.68 = (bf16[256,1152]{1,0:T(8,128)(2,1)S(1)}, bf16[256,1152]{1,0:T(8,128)(2,1)S(1)}) custom-call(f32[1]{0:T(128)S(6)} %copy.9.sharp_ref, f32[1]{0:T(128)S(6)} %copy.10.shift_ref, f32[1]{0:T(128)S(6)} %copy.11.adj_ref, bf16[256,1152]{1,0:T(8,128)(2,1)S(1)} %copy-done, bf16[256,1152]{1,0:T(8,128)(2,1)S(1)} %copy-done.1), custom_call_target="tpu_custom_call" | custom-call | flops 2717908992 | bytes 2359296 | tf_op jit(solution)/shard_map/pallas_call | solution.py:397
  71.1 0.8 %copy.12 = bf16[256,1152]{1,0:T(8,128)(2,1)} copy(bf16[256,1152]{1,0:T(8,128)(2,1)S(1)} %get-tuple-element.4) | data formatting | bytes 1179648
  71.9 0.8 %copy.13 = bf16[256,1152]{1,0:T(8,128)(2,1)} copy(bf16[256,1152]{1,0:T(8,128)(2,1)S(1)} %get-tuple-element.5) | data formatting | bytes 1179648
Async XLA Ops:
  2.6 1.1 %copy-start = (bf16[256,1152]{1,0:T(8,128)(2,1)S(1)}, bf16[256,1152]{1,0:T(8,128)(2,1)}, u32[]{:S(2)}) copy-start(bf16[256,1152]{1,0:T(8,128)(2,1)} %img_ref.1) | copy-start | bytes 1769476
  3.6 1.1 %copy-start.1 = (bf16[256,1152]{1,0:T(8,128)(2,1)S(1)}, bf16[256,1152]{1,0:T(8,128)(2,1)}, u32[]{:S(2)}) copy-start(bf16[256,1152]{1,0:T(8,128)(2,1)} %txt_ref.1) | copy-start | bytes 1769476

commit v3 on v2

--- a/solution.py
+++ b/solution.py
@@ -43,6 +43,7 @@
     send_sem,
     recv_sem,
     far_sem,
+    own_grad,
 ):
     blk = lax.axis_index("blk")
     grp = lax.axis_index("grp")
@@ -259,6 +260,16 @@
     def _():
         make_weights(0, ROWS, 2)
 
+    @pl.when(x < N_X - 1)
+    def _():
+        for h in range(2):
+            arrived(half(images, h, ROWS), 3 + h)
+        make_weights(ROWS, ROWS, 0)
+
+        @pl.when(core == 0)
+        def _():
+            make_weights(ROWS, ROWS, 2)
+
     send_text.wait_recv()
     share_near.start()
     @pl.when(x == 0)
@@ -281,14 +292,21 @@
         make_weights(0, ROWS, 3)
 
     for h in range(2):
-        arrived(half(images, h, ROWS), 3 + h)
         row = ROWS + h * HALF
-        make_weights(row, HALF, 0)
+
+        @pl.when(x == N_X - 1)
+        def _():
+            arrived(half(images, h, ROWS), 3 + h)
+            make_weights(row, HALF, 0)
+
+            @pl.when(core == 0)
+            def _():
+                make_weights(row, HALF, 2)
+
         make_weights(row, HALF, 1)
 
         @pl.when(core == 0)
         def _():
-            make_weights(row, HALF, 2)
             make_weights(row, HALF, 3)
             half(next_out, h)[...] = image_grad(row, HALF, 4).astype(jnp.bfloat16)
 
@@ -340,20 +358,17 @@
     share_part[0].wait_recv()
     grad_t = grad_t + part_in[0].astype(jnp.float32)
 
+    @pl.when(core == 0)
+    def _():
+        own_grad[...] = image_grad(0, ROWS, 2)
+
+    @pl.when(core == 1)
+    def _():
+        own_grad[...] = image_grad(0, ROWS, 4)
+
     for h in range(2):
         arrived(half(next_in, h), 7 + h)
-
-    @pl.when(core == 0)
-    def _():
-        gimg_ref[...] = (
-            image_grad(0, ROWS, 2) + next_in[...].astype(jnp.float32)
-        ).astype(jnp.bfloat16)
-
-    @pl.when(core == 1)
-    def _():
-        gimg_ref[...] = (
-            image_grad(0, ROWS, 4) + next_in[...].astype(jnp.float32)
-        ).astype(jnp.bfloat16)
+    gimg_ref[...] = (own_grad[...] + next_in[...].astype(jnp.float32)).astype(jnp.bfloat16)
 
     return_text.wait_recv()
     gtxt_ref[...] = (grad_t + text_in[...].astype(jnp.float32)).astype(jnp.bfloat16)
@@ -416,9 +431,10 @@
             pltpu.SemaphoreType.DMA((27,)),
             pltpu.SemaphoreType.DMA((14,)),
             pltpu.SemaphoreType.REGULAR,
+            pltpu.VMEM((ROWS, D), jnp.float32),
         ],
         compiler_params=pltpu.CompilerParams(
-            collective_id=0, has_side_effects=True, vmem_limit_bytes=48 << 20
+            collective_id=0, has_side_effects=True, vmem_limit_bytes=60 << 20
         ),
         cost_estimate=pl.CostEstimate(
             flops=18 * 2 * ROWS * ROWS * D, bytes_accessed=4 * ROWS * D * 2, transcendentals=6 * ROWS * ROWS

time: 73 us -> 73.7 us (level)
  the two profiles are of different devices: /device:TPU:1 before, /device:TPU:64 now
where the time goes in v3:
time: 73.7 us; the launch traced here: 73.5 us
  Pallas kernels  68.1 us (92%)
  local copies, waits for them, and re-layouts  2.8 us (4%)
  between operations  2.58 us (4%)
    pallas_call x1, Pallas kernels, on_device(): pl.pallas_call(kernel, out_shape=(shard, shard), in_specs=[pl.BlockSpec(m...  68.1 us
    unnamed x4, local copies, waits for them, and re-layouts  2.8 us

profile of v3, /device:TPU:64, one launch (start us, length us, event | category | flops | bytes accessed | tf_op | source)
XLA Modules:
  0.0 73.5 jit_solution(4739120156941505872)
XLA Ops:
  2.6 68.1 %shard_map.68 = (bf16[256,1152]{1,0:T(8,128)(2,1)}, bf16[256,1152]{1,0:T(8,128)(2,1)}) custom-call(f32[1]{0:T(128)S(6)} %copy.9.sharp_ref, f32[1]{0:T(128)S(6)} %copy.10.shift_ref, f32[1]{0:T(128)S(6)} %copy.11.adj_ref, bf16[256,1152]{1,0:T(8,128)(2,1)} %img_ref.1, bf16[256,1152]{1,0:T(8,128)(2,1)} %txt_ref.1), custom_call_target="tpu_custom_call" | custom-call | flops 2717908992 | bytes 2359296 | tf_op jit(solution)/shard_map/pallas_call | solution.py:412
  70.7 0.0 copy-start
  70.7 2.0 %copy.12 = bf16[256,1152]{1,0:T(8,128)(2,1)} copy(bf16[256,1152]{1,0:T(8,128)(2,1)} %get-tuple-element.4) | data formatting | bytes 1179648
  72.7 0.0 copy-done
  72.7 0.8 %copy.13 = bf16[256,1152]{1,0:T(8,128)(2,1)} copy(bf16[256,1152]{1,0:T(8,128)(2,1)S(1)} %copy-done) | data formatting | bytes 1179648
Async XLA Ops:
  70.7 2.0 %copy-start = (bf16[256,1152]{1,0:T(8,128)(2,1)S(1)}, bf16[256,1152]{1,0:T(8,128)(2,1)}, u32[]{:S(2)}) copy-start(bf16[256,1152]{1,0:T(8,128)(2,1)} %get-tuple-element.5) | copy-start | bytes 1769476

commit v4 on v2

--- a/solution.py
+++ b/solution.py
@@ -43,6 +43,7 @@
     send_sem,
     recv_sem,
     far_sem,
+    own_grad,
 ):
     blk = lax.axis_index("blk")
     grp = lax.axis_index("grp")
@@ -307,9 +308,8 @@
             grad_last[h].start()
 
     both = pl.multiple_of((1 - core) * ROWS, ROWS)
-    for t in (1, 0):
-        part_out[t] = text_grad(both, ROWS, 2 + t).astype(jnp.bfloat16)
-        share_part[t].start()
+    part_out[1] = text_grad(both, ROWS, 3).astype(jnp.bfloat16)
+    share_part[1].start()
     grad_near = text_grad(0, 2 * ROWS, 1)
     share_part[1].wait_recv()
     text_out[...] = (grad_near + part_in[1].astype(jnp.float32)).astype(jnp.bfloat16)
@@ -336,24 +336,23 @@
     def _():
         return_text.start()
 
+    part_out[0] = text_grad(both, ROWS, 2).astype(jnp.bfloat16)
+    share_part[0].start()
     grad_t = text_grad(0, 2 * ROWS, 0)
     share_part[0].wait_recv()
     grad_t = grad_t + part_in[0].astype(jnp.float32)
 
+    @pl.when(core == 0)
+    def _():
+        own_grad[...] = image_grad(0, ROWS, 2)
+
+    @pl.when(core == 1)
+    def _():
+        own_grad[...] = image_grad(0, ROWS, 4)
+
     for h in range(2):
         arrived(half(next_in, h), 7 + h)
-
-    @pl.when(core == 0)
-    def _():
-        gimg_ref[...] = (
-            image_grad(0, ROWS, 2) + next_in[...].astype(jnp.float32)
-        ).astype(jnp.bfloat16)
-
-    @pl.when(core == 1)
-    def _():
-        gimg_ref[...] = (
-            image_grad(0, ROWS, 4) + next_in[...].astype(jnp.float32)
-        ).astype(jnp.bfloat16)
+    gimg_ref[...] = (own_grad[...] + next_in[...].astype(jnp.float32)).astype(jnp.bfloat16)
 
     return_text.wait_recv()
     gtxt_ref[...] = (grad_t + text_in[...].astype(jnp.float32)).astype(jnp.bfloat16)
@@ -416,6 +415,7 @@
             pltpu.SemaphoreType.DMA((27,)),
             pltpu.SemaphoreType.DMA((14,)),
             pltpu.SemaphoreType.REGULAR,
+            pltpu.VMEM((ROWS, D), jnp.float32),
         ],
         compiler_params=pltpu.CompilerParams(
             collective_id=0, has_side_effects=True, vmem_limit_bytes=48 << 20

time: 73 us -> 73 us (level)
  no operation moved by 1% of the time
where the time goes in v4:
time: 73 us; the launch traced here: 72.7 us
  Pallas kernels  66.4 us (91%)
  local copies, waits for them, and re-layouts  3.75 us (5%)
  between operations  2.58 us (4%)
    pallas_call x1, Pallas kernels, on_device(): pl.pallas_call(kernel, out_shape=(shard, shard), in_specs=[pl.BlockSpec(m...  66.4 us
    unnamed x6, local copies, waits for them, and re-layouts  3.75 us

profile of v4, /device:TPU:1, one launch (start us, length us, event | category | flops | bytes accessed | tf_op | source)
XLA Modules:
  0.0 72.7 jit_solution(8882885563130761465)
XLA Ops:
  2.6 0.0 copy-start
  2.6 1.1 %copy-done = bf16[256,1152]{1,0:T(8,128)(2,1)S(1)} copy-done((bf16[256,1152]{1,0:T(8,128)(2,1)S(1)}, bf16[256,1152]{1,0:T(8,128)(2,1)}, u32[]{:S(2)}) %copy-start) | copy-done | bytes 589848
  3.6 0.0 copy-start.1
  3.6 1.1 %copy-done.1 = bf16[256,1152]{1,0:T(8,128)(2,1)S(1)} copy-done((bf16[256,1152]{1,0:T(8,128)(2,1)S(1)}, bf16[256,1152]{1,0:T(8,128)(2,1)}, u32[]{:S(2)}) %copy-start.1) | copy-done | bytes 589848
  4.7 66.4 %shard_map.68 = (bf16[256,1152]{1,0:T(8,128)(2,1)S(1)}, bf16[256,1152]{1,0:T(8,128)(2,1)S(1)}) custom-call(f32[1]{0:T(128)S(6)} %copy.9.sharp_ref, f32[1]{0:T(128)S(6)} %copy.10.shift_ref, f32[1]{0:T(128)S(6)} %copy.11.adj_ref, bf16[256,1152]{1,0:T(8,128)(2,1)S(1)} %copy-done, bf16[256,1152]{1,0:T(8,128)(2,1)S(1)} %copy-done.1), custom_call_target="tpu_custom_call" | custom-call | flops 2717908992 | bytes 2359296 | tf_op jit(solution)/shard_map/pallas_call | solution.py:396
  71.1 0.8 %copy.12 = bf16[256,1152]{1,0:T(8,128)(2,1)} copy(bf16[256,1152]{1,0:T(8,128)(2,1)S(1)} %get-tuple-element.4) | data formatting | bytes 1179648
  71.9 0.8 %copy.13 = bf16[256,1152]{1,0:T(8,128)(2,1)} copy(bf16[256,1152]{1,0:T(8,128)(2,1)S(1)} %get-tuple-element.5) | data formatting | bytes 1179648
Async XLA Ops:
  2.6 1.1 %copy-start = (bf16[256,1152]{1,0:T(8,128)(2,1)S(1)}, bf16[256,1152]{1,0:T(8,128)(2,1)}, u32[]{:S(2)}) copy-start(bf16[256,1152]{1,0:T(8,128)(2,1)} %img_ref.1) | copy-start | bytes 1769476
  3.6 1.1 %copy-start.1 = (bf16[256,1152]{1,0:T(8,128)(2,1)S(1)}, bf16[256,1152]{1,0:T(8,128)(2,1)}, u32[]{:S(2)}) copy-start(bf16[256,1152]{1,0:T(8,128)(2,1)} %txt_ref.1) | copy-start | bytes 1769476

commit v5 on v4

--- a/solution.py
+++ b/solution.py
@@ -242,17 +242,25 @@
     share_text.start()
 
     await_far()
-
-    @pl.when(x == 0)
-    def _():
-        for h in (0,):
-            image_first[h].start()
-
-    @pl.when(x > 0)
-    def _():
-        for h in (0,):
-            arrived(hop_img.at[h], 5 + h)
-            image_relay[h].start()
+    hold = (hi > 0, hi >= 0)
+
+    @pl.when((x == 0) & (jnp.logical_not(hold[0])))
+    def _():
+        image_first[0].start()
+
+    @pl.when((x > 0) & (jnp.logical_not(hold[0])))
+    def _():
+        arrived(hop_img.at[0], 5)
+        image_relay[0].start()
+
+    @pl.when((x == 0) & (jnp.logical_not(hold[1])))
+    def _():
+        image_first[1].start()
+
+    @pl.when((x > 0) & (jnp.logical_not(hold[1])))
+    def _():
+        arrived(hop_img.at[1], 6)
+        image_relay[1].start()
 
     share_text.wait_recv()
 
@@ -262,17 +270,24 @@
 
     send_text.wait_recv()
     share_near.start()
-    @pl.when(x == 0)
-    def _():
-        for h in (1,):
-            image_first[h].start()
-
-    @pl.when(x > 0)
-    def _():
-        for h in (1,):
-            arrived(hop_img.at[h], 5 + h)
-            image_relay[h].start()
-
+
+    @pl.when((x == 0) & (hold[0]))
+    def _():
+        image_first[0].start()
+
+    @pl.when((x > 0) & (hold[0]))
+    def _():
+        arrived(hop_img.at[0], 5)
+        image_relay[0].start()
+
+    @pl.when((x == 0) & (hold[1]))
+    def _():
+        image_first[1].start()
+
+    @pl.when((x > 0) & (hold[1]))
+    def _():
+        arrived(hop_img.at[1], 6)
+        image_relay[1].start()
 
     make_weights(0, ROWS, 1)
     share_near.wait_recv()
@@ -322,7 +337,9 @@
     def _():
         image_relay[1].wait_send()
 
-    @pl.when(grp_lo > 0)
+    late = (grp_lo == 0) & (hi == N_HI - 1)
+
+    @pl.when(jnp.logical_not(late))
     def _():
         return_text.start()
 
@@ -332,7 +349,7 @@
             arrived(hop_grad.at[h], 9 + h)
             grad_relay[h].start()
 
-    @pl.when(grp_lo == 0)
+    @pl.when(late)
     def _():
         return_text.start()
 
@@ -418,7 +435,7 @@
             pltpu.VMEM((ROWS, D), jnp.float32),
         ],
         compiler_params=pltpu.CompilerParams(
-            collective_id=0, has_side_effects=True, vmem_limit_bytes=48 << 20
+            collective_id=0, has_side_effects=True, vmem_limit_bytes=60 << 20
         ),
         cost_estimate=pl.CostEstimate(
             flops=18 * 2 * ROWS * ROWS * D, bytes_accessed=4 * ROWS * D * 2, transcendentals=6 * ROWS * ROWS

time: 73 us -> 73.2 us (level)
  local copies, waits for them, and re-layouts: 3.75 us -> 2.8 us
    unnamed x6 -> x4, local copies, waits for them, and re-layouts: 3.75 us -> 2.8 us
where the time goes in v5:
time: 73.2 us; the launch traced here: 72.4 us
  Pallas kernels  67 us (92%)
  local copies, waits for them, and re-layouts  2.8 us (4%)
  between operations  2.58 us (4%)
    pallas_call x1, Pallas kernels, on_device(): pl.pallas_call(kernel, out_shape=(shard, shard), in_specs=[pl.BlockSpec(m...  67 us
    unnamed x4, local copies, waits for them, and re-layouts  2.8 us

profile of v5, /device:TPU:1, one launch (start us, length us, event | category | flops | bytes accessed | tf_op | source)
XLA Modules:
  0.0 72.4 jit_solution(10052305357820998615)
XLA Ops:
  2.6 67.0 %shard_map.68 = (bf16[256,1152]{1,0:T(8,128)(2,1)}, bf16[256,1152]{1,0:T(8,128)(2,1)}) custom-call(f32[1]{0:T(128)S(6)} %copy.9.sharp_ref, f32[1]{0:T(128)S(6)} %copy.10.shift_ref, f32[1]{0:T(128)S(6)} %copy.11.adj_ref, bf16[256,1152]{1,0:T(8,128)(2,1)} %img_ref.1, bf16[256,1152]{1,0:T(8,128)(2,1)} %txt_ref.1), custom_call_target="tpu_custom_call" | custom-call | flops 2717908992 | bytes 2359296 | tf_op jit(solution)/shard_map/pallas_call | solution.py:413
  69.6 0.0 copy-start
  69.6 2.0 %copy.12 = bf16[256,1152]{1,0:T(8,128)(2,1)} copy(bf16[256,1152]{1,0:T(8,128)(2,1)} %get-tuple-element.4) | data formatting | bytes 1179648
  71.5 0.0 copy-done
  71.6 0.8 %copy.13 = bf16[256,1152]{1,0:T(8,128)(2,1)} copy(bf16[256,1152]{1,0:T(8,128)(2,1)S(1)} %copy-done) | data formatting | bytes 1179648
Async XLA Ops:
  69.6 2.0 %copy-start = (bf16[256,1152]{1,0:T(8,128)(2,1)S(1)}, bf16[256,1152]{1,0:T(8,128)(2,1)}, u32[]{:S(2)}) copy-start(bf16[256,1152]{1,0:T(8,128)(2,1)} %get-tuple-element.5) | copy-start | bytes 1769476
